TPU v7x, 512 devices: a whole 4x8x8 slice. The times are simulated.
512 devices in a mesh: row: 32 (over z_lo, y, core), col: 16 (over x, z_hi).
Axes of the slice: x: 4, y: 8, z: 8 (z_hi: 4, z_lo: 2; z = z_hi * 2 + z_lo), core: 2. Of those that a mesh axis runs over, the one named last changes fastest.
Arguments:
- pair: bfloat16 [512, 512, 128], P('row', 'col'), may hold values from -6 to 6
- pair_mask: int32 [512, 512], P('row', 'col'), may hold values 0 or 1
- gain_in: float32 [128], replicated, may hold values from 0.1 to 1.9
- w_in: bfloat16 [128, 512], replicated, may hold values from -0.5 to 0.5
- w_gate: bfloat16 [128, 128], replicated, may hold values from -0.5 to 0.5
- gain_mid: float32 [128], replicated, may hold values from 0.1 to 1.9
- w_out: bfloat16 [128, 128], replicated, may hold values from -0.5 to 0.5
Outputs:
- pair_out: bfloat16 [512, 512, 128], P('row', 'col')
All inputs are finite; a program needn't handle non-finite values. No bound on the sum of `pair_mask` on one device may be relied on, other than what follows from the above.
Results may differ from a plain program's by a relative error of at most 0.013.
Values may be sent and summed in bfloat16 or wider, within the bound.
No kernel may reach another device: no remote copies, remote signals or barrier semaphores. Data moves between devices by JAX's collectives and lax.ppermute only.
A program may use at most 64 MiB of HBM per device.

v0:
```python
import jax
import jax.numpy as jnp
from jax import lax
from jax.sharding import PartitionSpec as P


def layer_norm(values, scale):
    center = values - jnp.mean(values, axis=-1, keepdims=True)
    spread = jnp.mean(center * center, axis=-1, keepdims=True)
    return center * lax.rsqrt(spread + 1e-05) * scale


def triangle_inputs(pair, pair_mask, gain_in, w_in):
    width = pair.shape[-1]
    normed = layer_norm(pair.astype(jnp.float32), gain_in).astype(jnp.bfloat16)
    projected = jnp.dot(normed.reshape(-1, width), w_in, preferred_element_type=jnp.float32)
    projected = projected.reshape(pair.shape[0], pair.shape[1], 4 * width)
    keeper = pair_mask.astype(jnp.float32)[:, :, None]
    left_side = jax.nn.sigmoid(projected[..., :width]) * projected[..., width : 2 * width] * keeper
    right_side = (
        jax.nn.sigmoid(projected[..., 2 * width : 3 * width]) * projected[..., 3 * width :] * keeper
    )
    return (normed, left_side.astype(jnp.bfloat16), right_side.astype(jnp.bfloat16))


def triangle_output(pair, normed, summed, gain_mid, w_gate, w_out):
    width = pair.shape[-1]
    gating = jax.nn.sigmoid(
        jnp.dot(normed.reshape(-1, width), w_gate, preferred_element_type=jnp.float32)
    )
    middle = layer_norm(summed, gain_mid).astype(jnp.bfloat16).reshape(-1, width)
    update = gating * jnp.dot(middle, w_out, preferred_element_type=jnp.float32)
    result = pair.astype(jnp.float32).reshape(-1, width) + update
    return result.reshape(pair.shape).astype(jnp.bfloat16)


def shards(pair, pair_mask, gain_in, w_in, w_gate, gain_mid, w_out):
    normed, left_side, right_side = triangle_inputs(pair, pair_mask, gain_in, w_in)
    right_all = lax.all_gather(right_side, "row", axis=0, tiled=True)
    shares = lax.psum_scatter(
        jnp.einsum("jkc,ikc->jic", right_all, left_side, preferred_element_type=jnp.float32).astype(
            jnp.bfloat16
        ),
        "col",
        scatter_dimension=0,
        tiled=True,
    ).astype(jnp.float32)
    summed = jnp.transpose(shares, (1, 0, 2))
    return triangle_output(pair, normed, summed, gain_mid, w_gate, w_out)


def solution(mesh):
    in_specs = (P("row", "col", None), P("row", "col"), P(), P(), P(), P(), P())
    out_specs = P("row", "col", None)
    return jax.shard_map(shards, mesh=mesh, in_specs=in_specs, out_specs=out_specs, check_vma=False)
```

profile of v0, /device:TPU:1, one launch (start us, length us, event | category | flops | bytes accessed | tf_op | source)
XLA Modules:
  0.0 228.6 jit_solution(12852842399348484206)
XLA Ops:
  6.5 0.0 copy-start
  6.5 0.0 all-gather.2.cloned.1.call-start
  6.5 1.1 convert_reduce_fusion
  7.6 1.2 multiply_reduce_fusion
  8.8 0.7 convert_element_type.34
  9.5 1.1 multiply_convert_fusion
  10.6 0.3 fusion.20
  10.9 0.8 fusion.6
  11.7 0.0 all-gather.2.cloned.1.call-update
  11.8 0.0 reduce-scatter.2.cloned.1.call-start
  11.8 0.4 copy.13
  12.3 75.3 %all-gather.2.cloned.1.call-done = bf16[512,32,128]{2,1,0:T(8,128)(2,1)} async-done(((bf16[16,32,128]{2,1,0:T(8,128)(2,1)}), bf16[512,32,128]{2,1,0:T(8,128)(2,1)}) %all-gather.2.cloned.1.call-update) | async-done | bytes 4194320 | tf_op jit(solution)/shard_map/all_gather | solution.py:39
  87.6 23.0 %copy.14 = bf16[512,32,128]{1,0,2:T(8,128)(2,1)} copy(bf16[512,32,128]{2,1,0:T(8,128)(2,1)} %all-gather.2.cloned.1.call-done) | data formatting | bytes 8388608 | tf_op jit(solution)/shard_map/all_gather | solution.py:39
  110.6 10.2 %convert_bitcast_fusion = bf16[512,16,128]{0,1,2:T(8,128)(2,1)S(1)} fusion(bf16[16,32,128]{1,0,2:T(8,128)(2,1)S(1)} %copy.13, bf16[512,32,128]{1,0,2:T(8,128)(2,1)} %copy.14), kind=kOutput, calls=%fused_computation | convolution fusion | flops 68157440 | bytes 6422528 | tf_op jit(solution)/shard_map/jkc,ikc->jic/dot_general | solution.py:41
  120.8 0.0 copy-start.1
  120.9 0.0 copy-start.2
  120.9 3.9 %copy.15 = bf16[512,16,128]{2,1,0:T(8,128)(2,1)} copy(bf16[512,16,128]{0,1,2:T(8,128)(2,1)S(1)} %convert_bitcast_fusion) | data formatting | bytes 4194304 | tf_op jit(solution)/shard_map/convert_element_type | solution.py:41
  124.8 0.0 reduce-scatter.2.cloned.1.call-update
  124.8 0.2 fusion.3
  125.1 92.5 %reduce-scatter.2.cloned.1.call-done = bf16[32,16,128]{2,1,0:T(8,128)(2,1)} async-done(((bf16[512,16,128]{2,1,0:T(8,128)(2,1)}), bf16[32,16,128]{2,1,0:T(8,128)(2,1)}) %reduce-scatter.2.cloned.1.call-update) | async-done | bytes 131088 | tf_op jit(solution)/shard_map/reduce_scatter | solution.py:40
  217.6 1.0 bitcast_reduce_fusion
  218.6 1.2 fusion.17
  219.8 1.1 fusion.19
  221.0 0.8 fusion.4
  (11 shorter events, 0.0 us)
Async XLA Ops:
  6.5 4.1 %copy-start = (bf16[128,512]{1,0:T(8,128)(2,1)S(1)}, bf16[128,512]{1,0:T(8,128)(2,1)}, u32[]{:S(2)}) copy-start(bf16[128,512]{1,0:T(8,128)(2,1)} %param.10) | copy-start | bytes 393220
  6.5 81.1 %all-gather.2.cloned.1.call-start = ((), (), s32[]{:S(2)}) async-start(), calls=%async_computation.1 | async-start | bytes 4325376 | tf_op jit(solution)/shard_map/all_gather | solution.py:39
  11.8 205.8 %reduce-scatter.2.cloned.1.call-start = ((), (), s32[]{:S(2)}) async-start(), calls=%async_computation.2 | async-start | bytes 2228224 | tf_op jit(solution)/shard_map/reduce_scatter | solution.py:40
  120.8 4.0 %copy-start.4 = (bf16[128,128]{1,0:T(8,128)(2,1)S(1)}, bf16[128,128]{1,0:T(8,128)(2,1)}, u32[]{:S(2)}) copy-start(bf16[128,128]{1,0:T(8,128)(2,1)} %param.11) | copy-start | bytes 98308
  120.8 99.0 %copy-start.3 = (f32[128]{0:T(128)S(1)}, f32[128]{0:T(128)}, u32[]{:S(2)}) copy-start(f32[128]{0:T(128)} %param.12) | copy-start | bytes 1540
  120.8 100.1 %copy-start.1 = (bf16[16,32,128]{2,1,0:T(8,128)(2,1)S(1)}, bf16[16,32,128]{2,1,0:T(8,128)(2,1)}, u32[]{:S(2)}) copy-start(bf16[16,32,128]{2,1,0:T(8,128)(2,1)} %param.7) | copy-start | bytes 393220
  120.9 100.1 %copy-start.2 = (bf16[128,128]{1,0:T(8,128)(2,1)S(1)}, bf16[128,128]{1,0:T(8,128)(2,1)}, u32[]{:S(2)}) copy-start(bf16[128,128]{1,0:T(8,128)(2,1)} %param.13) | copy-start | bytes 98308
Sparse Core Ops, SparseCore 0:
  11.9 75.6 all-gather.1
  124.9 92.5 reduce-scatter.1
where the time goes:
time: 229 us
  waiting for transfers between devices  168 us (73%)
  local copies, waits for them, and re-layouts  27.4 us (12%)
  between operations  13.6 us (6%)
  matrix products  11.5 us (5%)
  other arithmetic  8.2 us (4%)
    reduce_scatter x1, waiting for transfers between devices, shards(): lax.psum_scatter(jnp.einsum('jkc,ikc->jic', right_all, left_side, preferr...  92.5 us
    all_gather x1, waiting for transfers between devices, shards(): right_all = lax.all_gather(right_side, 'row', axis=0, tiled=True)  75.3 us
    all_gather x1, local copies, waits for them, and re-layouts, shards(): right_all = lax.all_gather(right_side, 'row', axis=0, tiled=True)  23 us
    dot_general x1, matrix products, shards(): jnp.einsum('jkc,ikc->jic', right_all, left_side, preferred_element_type=j...  10.2 us
  transfers between devices with their start and end apart: 2, of which 2 were waited for; matrix products, arithmetic and copies ran while one was open for 0% of the time, Pallas kernels for 0%

commit v1 on v0

v1 whole, which is shorter than its diff:
```python
import jax
import jax.numpy as jnp
from jax import lax
from jax.experimental import pallas as pl
from jax.experimental.pallas import tpu as pltpu
from jax.sharding import Mesh
from jax.sharding import PartitionSpec as P

AXES = ("z_lo", "y", "core", "x", "z_hi")
ORDER = ("x", "z_hi", "core", "z_lo", "y")
F32, BF16 = jnp.float32, jnp.bfloat16


def iota(shape, axis):
    return lax.broadcasted_iota(jnp.int32, shape, axis)


def project(pair_ref, mask_ref, gain_ref, w_in_ref, w_gate_ref, send_ref, gate_ref):
    values = pair_ref[...].astype(F32)
    center = values - jnp.mean(values, axis=-1, keepdims=True)
    spread = jnp.mean(center * center, axis=-1, keepdims=True)
    normed = (center * lax.rsqrt(spread + 1e-05) * gain_ref[...]).astype(BF16)
    gate_ref[...] = jax.nn.sigmoid(jnp.dot(normed, w_gate_ref[...], preferred_element_type=F32))
    tokens = jnp.concatenate(
        [
            normed[core * 256 + i * 32 + half * 16 :][:16]
            for core in range(2)
            for half in range(2)
            for i in range(8)
        ],
        axis=0,
    )
    place = iota((32, 512), 1)
    column = (place >> 7 & 1) * 16 + (place & 15)
    spread_mask = jnp.dot(
        mask_ref[...].astype(F32), (column == iota((32, 512), 0)).astype(F32), preferred_element_type=F32
    )
    place = iota((16, 512), 1)
    row = (place >> 8) * 8 + (place >> 4 & 7)
    keeper = jnp.sum(jnp.where(row == iota((16, 512), 0), spread_mask, 0.0), axis=0, keepdims=True)
    projected = lax.dot_general(w_in_ref[...], tokens, (((0,), (1,)), ((), ())), preferred_element_type=F32)
    for side in range(2):
        start = side * 256
        both = (
            jax.nn.sigmoid(projected[start : start + 128]) * projected[start + 128 : start + 256] * keeper
        )
        for q in range(16):
            block = both[q * 8 : q * 8 + 8]
            for core in range(2):
                two = jnp.concatenate(
                    [block[:, core * 256 : core * 256 + 128], block[:, core * 256 + 128 : core * 256 + 256]], axis=0
                )
                send_ref[q * 32 + core * 16 : q * 32 + core * 16 + 16, side * 128 : side * 128 + 128] = two.astype(BF16)


def assemble(got_ref, left_ref, right_ref):
    for i in range(8):
        left_ref[i * 32 : i * 32 + 32, :] = jnp.concatenate(
            [got_ref[q * 32 : q * 32 + 32, i * 16 : i * 16 + 16] for q in range(16)], axis=1
        )
    right = jnp.concatenate(
        [
            jnp.concatenate(
                [got_ref[q * 32 : q * 32 + 32, 128 + j * 16 : 128 + j * 16 + 16] for q in range(16)], axis=1
            )
            for j in range(8)
        ],
        axis=0,
    )
    to, source = iota((256, 256), 0), iota((256, 256), 1)
    moved = ((to & 7) * 32 + (to >> 3 & 1) * 16 + (to >> 4)) == source
    right_ref[...] = jnp.dot(moved.astype(BF16), right, preferred_element_type=F32).astype(BF16)


def multiply(left_ref, right_ref, send_ref):
    summed = lax.dot_general(
        left_ref[...], right_ref[...], (((1,), (1,)), ((), ())), preferred_element_type=F32
    ).astype(BF16)
    for q in range(16):
        send_ref[q * 32 : q * 32 + 32, :] = jnp.concatenate(
            [summed[i * 32 : i * 32 + 32, q * 16 : q * 16 + 16] for i in range(16)], axis=1
        )


def finish(got_ref, pair_ref, gate_ref, gain_ref, w_out_ref, out_ref):
    same = iota((128, 128), 0) == iota((128, 128), 1)
    gain = jnp.sum(jnp.where(same, gain_ref[...], 0.0), axis=1, keepdims=True)
    updates = []
    for core in range(2):
        parts = []
        for q in range(16):
            two = got_ref[q * 32 + core * 16 : q * 32 + core * 16 + 16, :].astype(F32)
            parts.append(two[:8] + two[8:])
        summed = jnp.concatenate(parts, axis=0)
        center = summed - jnp.mean(summed, axis=0, keepdims=True)
        spread = jnp.mean(center * center, axis=0, keepdims=True)
        middle = (center * lax.rsqrt(spread + 1e-05) * gain).astype(BF16)
        updates.append(
            lax.dot_general(middle, w_out_ref[...], (((0,), (0,)), ((), ())), preferred_element_type=F32)
        )
    update = jnp.concatenate(
        [updates[core][at * 8 : at * 8 + 8] for at in range(32) for core in range(2)], axis=0
    )
    out_ref[...] = (pair_ref[...].astype(F32) + gate_ref[...] * update).astype(BF16)


def kernel(body, out_shape):
    return pl.pallas_call(
        body, out_shape=out_shape, compiler_params=pltpu.CompilerParams(vmem_limit_bytes=32 * 1024 * 1024)
    )


def exchange(rows):
    return lax.all_to_all(rows.reshape(512, 2, 128), ORDER, 0, 0).reshape(512, 256)


def shards(pair, pair_mask, gain_in, w_in, w_gate, gain_mid, w_out):
    tokens = pair.reshape(512, 128)
    array = jax.ShapeDtypeStruct
    sides, gate = kernel(project, (array((512, 256), BF16), array((512, 128), F32)))(
        tokens, pair_mask, gain_in.reshape(1, 128), w_in, w_gate
    )
    left, right = kernel(assemble, (array((256, 256), BF16), array((256, 256), BF16)))(exchange(sides))
    left = lax.all_gather(left, "core", axis=0, tiled=True)
    parts = kernel(multiply, array((512, 256), BF16))(left, right)
    out = kernel(finish, array((512, 128), BF16))(exchange(parts), tokens, gate, gain_mid.reshape(1, 128), w_out)
    return out.reshape(pair.shape)


def solution(mesh):
    fine = Mesh(mesh.devices.reshape(2, 8, 2, 4, 4), AXES)
    pair_spec = P(AXES[:3], AXES[3:], None)
    in_specs = (pair_spec, P(AXES[:3], AXES[3:]), P(), P(), P(), P(), P())
    return jax.shard_map(shards, mesh=fine, in_specs=in_specs, out_specs=pair_spec, check_vma=False)
```

time: 229 us -> 75.2 us (0.33)
  waiting for transfers between devices: 168 us -> 0 us
  blocking collectives: 0 us -> 66.9 us
  local copies, waits for them, and re-layouts: 27.4 us -> 4.98 us
  between operations: 13.6 us -> 0.06 us
  matrix products: 11.5 us -> 0 us
  other arithmetic: 8.2 us -> 0 us
  Pallas kernels: 0 us -> 2.95 us
    reduce_scatter x1 -> x0, waiting for transfers between devices: 92.5 us -> none  [shards(): lax.psum_scatter(jnp.einsum('jkc,ikc->jic', right_all, left_side, preferr...]
    all_gather x1 -> x0, waiting for transfers between devices: 75.3 us -> none  [shards(): right_all = lax.all_gather(right_side, 'row', axis=0, tiled=True)]
    all_to_all x0 -> x2, blocking collectives: none -> 64.1 us  [exchange(): lax.all_to_all(rows.reshape(512, 2, 128), ORDER, 0, 0).reshape(512, 256)]
    all_gather x1 -> x0, local copies, waits for them, and re-layouts: 23 us -> none  [shards(): right_all = lax.all_gather(right_side, 'row', axis=0, tiled=True)]
    dot_general x4 -> x0, matrix products: 11.5 us -> none  [the longest x1 10.2 us: shards(): jnp.einsum('jkc,ikc->jic', right_all, left_side, preferred_element_type=j...]
    unnamed x10 -> x18, local copies, waits for them, and re-layouts: 0.03 us -> 4.85 us
    reduce_sum x4 -> x0, other arithmetic: 4.44 us -> none  [the longest x2 2.32 us: layer_norm(): spread = jnp.mean(center * center, axis=-1, keepdims=True)]
    convert_element_type x2 -> x0, local copies, waits for them, and re-layouts: 4.35 us -> none  [the longest x1 3.92 us: shards(): jnp.einsum('jkc,ikc->jic', right_all, left_side, preferred_element_type=j...]
  transfers between devices with their start and end apart: 2 -> 0, of which waited for: 2 -> 0; matrix products, arithmetic and copies ran while one was open for 0% -> 0% of each run, Pallas kernels for 0% -> 0%
where the time goes in v1:
time: 75.2 us; the launch traced here: 74.9 us
  blocking collectives  66.9 us (89%)
  local copies, waits for them, and re-layouts  4.98 us (7%)
  Pallas kernels  2.95 us (4%)
    all_to_all x2, blocking collectives, exchange(): lax.all_to_all(rows.reshape(512, 2, 128), ORDER, 0, 0).reshape(512, 256)  64.1 us
    unnamed x18, local copies, waits for them, and re-layouts  4.85 us
    all_gather x1, blocking collectives, shards(): left = lax.all_gather(left, 'core', axis=0, tiled=True)  2.79 us

profile of v1, /device:TPU:1, one launch (start us, length us, event | category | flops | bytes accessed | tf_op | source)
XLA Modules:
  0.0 74.9 jit_solution(7152225334189787430)
XLA Ops:
  0.0 0.0 copy-start.6
  0.0 0.7 copy-done.6
  0.7 0.0 copy-start
  0.7 0.9 %copy-done = bf16[16,32,128]{2,1,0:T(8,128)(2,1)S(1)} copy-done((bf16[16,32,128]{2,1,0:T(8,128)(2,1)S(1)}, bf16[16,32,128]{2,1,0:T(8,128)(2,1)}, u32[]{:S(2)}) %copy-start) | copy-done | bytes 131096
  1.6 0.0 copy-start.2
  1.6 0.9 %copy-done.2 = bf16[128,512]{1,0:T(8,128)(2,1)S(1)} copy-done((bf16[128,512]{1,0:T(8,128)(2,1)S(1)}, bf16[128,512]{1,0:T(8,128)(2,1)}, u32[]{:S(2)}) %copy-start.2) | copy-done | bytes 131096
  2.5 0.0 copy-start.3
  2.5 0.8 %copy-done.3 = bf16[128,128]{1,0:T(8,128)(2,1)S(1)} copy-done((bf16[128,128]{1,0:T(8,128)(2,1)S(1)}, bf16[128,128]{1,0:T(8,128)(2,1)}, u32[]{:S(2)}) %copy-start.3) | copy-done | bytes 32792
  3.2 0.0 copy-start.5
  3.2 0.7 copy-done.5
  3.9 0.5 shard_map.73
  4.5 0.1 reshape.26
  4.5 38.5 %all_to_all.10 = bf16[512,2,128]{2,1,0:T(2,128)(2,1)S(1)} all-to-all(bf16[512,2,128]{2,1,0:T(2,128)(2,1)S(1)} %reshape.26), channel_id=1, replica_groups=mesh['z_lo'=2,'y'=8,'core'=2,'x'=4,'z_hi'=4] {'x','z_hi','core','z_lo','y'}, dimensions={0} | all-to-all | bytes 524288 | tf_op jit(solution)/shard_map/all_to_all | solution.py:114
  43.1 0.7 shard_map.74
  43.8 2.8 %all_gather.3.left_ref = bf16[512,256]{1,0:T(8,128)(2,1)S(1)} all-gather(bf16[256,256]{1,0:T(8,128)(2,1)S(1)} %get-tuple-element.10), channel_id=1, replica_groups=mesh['z_lo'=2,'y'=8,'core'=2,'x'=4,'z_hi'=4] {'core'}, dimensions={0}, use_global_device_ids=true | all-gather | bytes 393216 | tf_op jit(solution)/shard_map/all_gather | solution.py:124
  46.6 0.7 shard_map.75
  47.3 0.1 reshape.28
  47.4 25.6 %all_to_all.11 = bf16[512,2,128]{2,1,0:T(2,128)(2,1)S(1)} all-to-all(bf16[512,2,128]{2,1,0:T(2,128)(2,1)S(1)} %reshape.28), channel_id=1, replica_groups=mesh['z_lo'=2,'y'=8,'core'=2,'x'=4,'z_hi'=4] {'x','z_hi','core','z_lo','y'}, dimensions={0} | all-to-all | bytes 524288 | tf_op jit(solution)/shard_map/all_to_all | solution.py:114
  73.0 0.0 copy-start.1
  73.1 0.0 copy-start.7
  73.1 0.8 %copy-done.1 = bf16[16,32,128]{2,1,0:T(8,128)(2,1)S(1)} copy-done((bf16[16,32,128]{2,1,0:T(8,128)(2,1)S(1)}, bf16[16,32,128]{2,1,0:T(8,128)(2,1)}, u32[]{:S(2)}) %copy-start.1) | copy-done | bytes 131096
  73.9 0.0 copy-done.4
  73.9 0.0 copy-done.7
  73.9 1.0 %shard_map.76 = bf16[512,128]{1,0:T(8,128)(2,1)} custom-call(bf16[512,256]{1,0:T(8,128)(2,1)S(1)} %bitcast.13, bf16[512,128]{1,0:T(8,128)(2,1)S(1)} %bitcast.15, f32[512,128]{1,0:T(8,128)S(1)} %get-tuple-element.12.gate_ref, f32[1,128]{1,0:T(1,128)S(1)} %bitcast.17, bf16[128,128]{1,0:T(8,128)(2,1)S(1)} %copy-done.4), custom_call_target="tpu_custom_call" | custom-call | tf_op jit(solution)/shard_map/pallas_call | solution.py:126
  (3 shorter events, 0.1 us)
Async XLA Ops:
  0.0 0.7 copy-start.6
  0.7 0.9 %copy-start = (bf16[16,32,128]{2,1,0:T(8,128)(2,1)S(1)}, bf16[16,32,128]{2,1,0:T(8,128)(2,1)}, u32[]{:S(2)}) copy-start(bf16[16,32,128]{2,1,0:T(8,128)(2,1)} %param.7) | copy-start | bytes 393220
  1.6 0.9 %copy-start.2 = (bf16[128,512]{1,0:T(8,128)(2,1)S(1)}, bf16[128,512]{1,0:T(8,128)(2,1)}, u32[]{:S(2)}) copy-start(bf16[128,512]{1,0:T(8,128)(2,1)} %w_in_ref.1) | copy-start | bytes 393220
  2.5 0.8 %copy-start.3 = (bf16[128,128]{1,0:T(8,128)(2,1)S(1)}, bf16[128,128]{1,0:T(8,128)(2,1)}, u32[]{:S(2)}) copy-start(bf16[128,128]{1,0:T(8,128)(2,1)} %w_gate_ref.1) | copy-start | bytes 98308
  3.2 0.7 copy-start.5
  73.0 0.9 %copy-start.1 = (bf16[16,32,128]{2,1,0:T(8,128)(2,1)S(1)}, bf16[16,32,128]{2,1,0:T(8,128)(2,1)}, u32[]{:S(2)}) copy-start(bf16[16,32,128]{2,1,0:T(8,128)(2,1)} %param.7) | copy-start | bytes 393220
  73.0 0.9 %copy-start.4 = (bf16[128,128]{1,0:T(8,128)(2,1)S(1)}, bf16[128,128]{1,0:T(8,128)(2,1)}, u32[]{:S(2)}) copy-start(bf16[128,128]{1,0:T(8,128)(2,1)} %w_out_ref.1) | copy-start | bytes 98308
  73.1 0.9 %copy-start.7 = (f32[128]{0:T(128)S(1)}, f32[128]{0:T(128)}, u32[]{:S(2)}) copy-start(f32[128]{0:T(128)} %param.12) | copy-start | bytes 1540

commit v2 on v0

v2 whole, which is shorter than its diff:
```python
import jax
import jax.numpy as jnp
from jax import lax
from jax.experimental import pallas as pl
from jax.experimental.pallas import tpu as pltpu
from jax.sharding import Mesh
from jax.sharding import PartitionSpec as P

AXES = ("z_lo", "y", "core", "x", "z_hi")
F32, BF16 = jnp.float32, jnp.bfloat16


def iota(shape, axis):
    return lax.broadcasted_iota(jnp.int32, shape, axis)


def project(*refs):
    sources, (send_ref, gate_ref, pair_ref, gain_mid_ref, w_out_ref) = refs[:7], refs[7:12]
    mask_ref, gain_ref, w_in_ref, w_gate_ref, arrived = refs[12:]
    targets = (pair_ref, mask_ref, gain_ref, w_in_ref, w_gate_ref, gain_mid_ref, w_out_ref)
    copies = [
        pltpu.make_async_copy(source, target, arrived.at[n]) for n, (source, target) in enumerate(zip(sources, targets))
    ]
    for copy in copies:
        copy.start()
    for copy in copies:
        copy.wait()
    values = pair_ref[...].astype(F32)
    center = values - jnp.mean(values, axis=-1, keepdims=True)
    spread = jnp.mean(center * center, axis=-1, keepdims=True)
    normed = (center * lax.rsqrt(spread + 1e-05) * gain_ref[...]).astype(BF16)
    gate_ref[...] = jax.nn.sigmoid(jnp.dot(normed, w_gate_ref[...], preferred_element_type=F32))
    place = iota((32, 512), 1)
    spread_mask = jnp.dot(
        mask_ref[...].astype(F32), (place & 31 == iota((32, 512), 0)).astype(F32), preferred_element_type=F32
    )
    row = iota((16, 512), 1) >> 5
    keeper = jnp.sum(jnp.where(row == iota((16, 512), 0), spread_mask, 0.0), axis=0, keepdims=True)
    projected = lax.dot_general(w_in_ref[...], normed, (((0,), (1,)), ((), ())), preferred_element_type=F32)
    for side in range(2):
        start = side * 256
        both = (
            jax.nn.sigmoid(projected[start : start + 128]) * projected[start + 128 : start + 256] * keeper
        ).astype(BF16)
        for half in range(2):
            at = side * 1024 + half * 512
            send_ref[:, at : at + 512] = both[half * 64 : half * 64 + 64]


def turn(blocks, width):
    rows, lanes = blocks.shape
    return jnp.concatenate(
        [
            jnp.concatenate([blocks[a : a + 16, b : b + width] for a in range(0, rows, 16)], axis=1)
            for b in range(0, lanes, width)
        ],
        axis=0,
    )


def assemble(got_ref, left_ref, right_ref):
    left_ref[...] = jnp.concatenate([turn(got_ref[:, at : at + 512], 32) for at in (0, 512)], axis=1)
    right = jnp.concatenate([turn(got_ref[:, at : at + 512], 32) for at in (1024, 1536)], axis=1)
    to, source = iota((256, 256), 0), iota((256, 256), 1)
    moved = ((to & 15) * 16 + (to >> 4) == source).astype(BF16)
    right_ref[...] = jnp.dot(moved, right, preferred_element_type=F32).astype(BF16)


def multiply(left_ref, right_ref, send_ref):
    for half in range(2):
        channel = slice(half * 128, half * 128 + 128)
        summed = lax.dot_general(
            left_ref[:, channel], right_ref[:, channel], (((1,), (1,)), ((), ())), preferred_element_type=F32
        ).astype(BF16)
        for parity in range(2):
            at = half * 512 + parity * 256
            send_ref[:, at : at + 256] = turn(summed[:, parity * 256 : parity * 256 + 256], 16)


def finish(got_ref, pair_ref, gate_ref, gain_ref, w_out_ref, out_ref):
    same = iota((128, 128), 0) == iota((128, 128), 1)
    gain = jnp.sum(jnp.where(same, gain_ref[...], 0.0), axis=1, keepdims=True)
    parts = []
    for x in range(4):
        four = [got_ref[x * 64 + part * 16 : x * 64 + part * 16 + 16, :].astype(F32) for part in range(4)]
        parts.append((four[0] + four[1]) + (four[2] + four[3]))
    summed = jnp.concatenate([part[:, at : at + 512] for at in (0, 512) for part in parts], axis=0)
    center = summed - jnp.mean(summed, axis=0, keepdims=True)
    spread = jnp.mean(center * center, axis=0, keepdims=True)
    middle = (center * lax.rsqrt(spread + 1e-05) * gain).astype(BF16)
    update = lax.dot_general(middle, w_out_ref[...], (((0,), (0,)), ((), ())), preferred_element_type=F32)
    update = jnp.concatenate(
        [update[parity * 256 + i * 16 : parity * 256 + i * 16 + 16] for i in range(16) for parity in range(2)], axis=0
    )
    out_ref[...] = (pair_ref[...].astype(F32) + gate_ref[...] * update).astype(BF16)


def kernel(body, out_shape, **more):
    return pl.pallas_call(
        body, out_shape=out_shape, compiler_params=pltpu.CompilerParams(vmem_limit_bytes=32 * 1024 * 1024), **more
    )


def exchange(rows, axes):
    many, lanes = rows.shape
    return lax.all_to_all(rows.reshape(many, lanes // 128, 128), axes, 0, 0).reshape(many, lanes)


def shards(pair, pair_mask, gain_in, w_in, w_gate, gain_mid, w_out):
    array = jax.ShapeDtypeStruct
    sides, gate, tokens, gain_mid, w_out = kernel(
        project,
        (
            array((64, 2048), BF16),
            array((512, 128), F32),
            array((512, 128), BF16),
            array((1, 128), F32),
            array((128, 128), BF16),
        ),
        in_specs=[pl.BlockSpec(memory_space=pltpu.HBM)] * 7,
        scratch_shapes=[
            pltpu.VMEM((16, 32), jnp.int32),
            pltpu.VMEM((1, 128), F32),
            pltpu.VMEM((128, 512), BF16),
            pltpu.VMEM((128, 128), BF16),
            pltpu.SemaphoreType.DMA((7,)),
        ],
    )(
        *(
            pltpu.with_memory_space_constraint(value, pltpu.HBM)
            for value in (
                pair.reshape(512, 128),
                pair_mask,
                gain_in.reshape(1, 128),
                w_in,
                w_gate,
                gain_mid.reshape(1, 128),
                w_out,
            )
        )
    )
    left, right = kernel(assemble, (array((256, 256), BF16), array((256, 256), BF16)))(
        exchange(sides, ("x", "z_lo", "y"))
    )
    right = lax.all_gather(right, "core", axis=0, tiled=True)
    parts = kernel(multiply, array((256, 1024), BF16))(left, right)
    out = kernel(finish, array((512, 128), BF16))(exchange(parts, ("x", "z_hi", "z_lo", "y")), tokens, gate, gain_mid, w_out)
    return out.reshape(pair.shape)


def solution(mesh):
    fine = Mesh(mesh.devices.reshape(2, 8, 2, 4, 4), AXES)
    pair_spec = P(AXES[:3], AXES[3:], None)
    in_specs = (pair_spec, P(AXES[:3], AXES[3:]), P(), P(), P(), P(), P())
    return jax.shard_map(shards, mesh=fine, in_specs=in_specs, out_specs=pair_spec, check_vma=False)
```

time: 229 us -> 68.4 us (0.30)
  waiting for transfers between devices: 168 us -> 0 us
  blocking collectives: 0 us -> 63.2 us
  local copies, waits for them, and re-layouts: 27.4 us -> 0.29 us
  between operations: 13.6 us -> 0.05 us
  matrix products: 11.5 us -> 0 us
  other arithmetic: 8.2 us -> 0 us
  Pallas kernels: 0 us -> 4.11 us
    reduce_scatter x1 -> x0, waiting for transfers between devices: 92.5 us -> none  [shards(): lax.psum_scatter(jnp.einsum('jkc,ikc->jic', right_all, left_side, preferr...]
    all_gather x1 -> x0, waiting for transfers between devices: 75.3 us -> none  [shards(): right_all = lax.all_gather(right_side, 'row', axis=0, tiled=True)]
    all_to_all x0 -> x2, blocking collectives: none -> 58.5 us  [exchange(): lax.all_to_all(rows.reshape(many, lanes // 128, 128), axes, 0, 0)]
    all_gather x1 -> x0, local copies, waits for them, and re-layouts: 23 us -> none  [shards(): right_all = lax.all_gather(right_side, 'row', axis=0, tiled=True)]
    dot_general x4 -> x0, matrix products: 11.5 us -> none  [the longest x1 10.2 us: shards(): jnp.einsum('jkc,ikc->jic', right_all, left_side, preferred_element_type=j...]
    all_gather x0 -> x1, blocking collectives: none -> 4.7 us  [shards(): right = lax.all_gather(right, 'core', axis=0, tiled=True)]
    reduce_sum x4 -> x0, other arithmetic: 4.44 us -> none  [the longest x2 2.32 us: layer_norm(): spread = jnp.mean(center * center, axis=-1, keepdims=True)]
    convert_element_type x2 -> x0, local copies, waits for them, and re-layouts: 4.35 us -> none  [the longest x1 3.92 us: shards(): jnp.einsum('jkc,ikc->jic', right_all, left_side, preferred_element_type=j...]
  transfers between devices with their start and end apart: 2 -> 0, of which waited for: 2 -> 0; matrix products, arithmetic and copies ran while one was open for 0% -> 0% of each run, Pallas kernels for 0% -> 0%
where the time goes in v2:
time: 68.4 us; the launch traced here: 67.7 us
  blocking collectives  63.2 us (92%)
  Pallas kernels  4.11 us (6%)
    all_to_all x2, blocking collectives, exchange(): lax.all_to_all(rows.reshape(many, lanes // 128, 128), axes, 0, 0)  58.5 us
    all_gather x1, blocking collectives, shards(): right = lax.all_gather(right, 'core', axis=0, tiled=True)  4.7 us
    pallas_call x1, Pallas kernels, shards(): kernel(project, (array((64, 2048), BF16), array((512, 128), F32), array((...  1.6 us

profile of v2, /device:TPU:1, one launch (start us, length us, event | category | flops | bytes accessed | tf_op | source)
XLA Modules:
  0.0 67.7 jit_solution(6497162597939671636)
XLA Ops:
  0.0 1.6 %shard_map.73 = (bf16[64,2048]{1,0:T(8,128)(2,1)S(1)}, f32[512,128]{1,0:T(8,128)S(1)}, bf16[512,128]{1,0:T(8,128)(2,1)S(1)}, f32[1,128]{1,0:T(1,128)S(1)}, bf16[128,128]{1,0:T(8,128)(2,1)S(1)}) custom-call(bf16[512,128]{1,0:T(8,128)(2,1)} %bitcast.24, s32[16,32]{1,0:T(8,128)} %refs_1_.1, f32[1,128]{1,0:T(1,128)} %bitcast.25, bf16[128,512]{1,0:T(8,128)(2,1)} %refs_3_.1, ...), custom_call_target="tpu_custom_call" | custom-call | tf_op jit(solution)/shard_map/pallas_call | solution.py:111
  1.6 24.2 %all_to_all.10 = bf16[64,16,128]{2,1,0:T(8,128)(2,1)S(1)} all-to-all(bf16[64,16,128]{2,1,0:T(8,128)(2,1)S(1)} %bitcast.22), channel_id=1, replica_groups=mesh['z_lo'=2,'y'=8,'core'=2,'x'=4,'z_hi'=4] {'x','z_lo','y'}, dimensions={0} | all-to-all | bytes 524288 | tf_op jit(solution)/shard_map/all_to_all | solution.py:106
  25.9 0.1 copy.15
  26.0 0.3 shard_map.74
  26.3 4.7 %all_gather.3.right_ref = bf16[512,256]{1,0:T(8,128)(2,1)S(1)} all-gather(bf16[256,256]{1,0:T(8,128)(2,1)S(1)} %get-tuple-element.14), channel_id=1, replica_groups=mesh['z_lo'=2,'y'=8,'core'=2,'x'=4,'z_hi'=4] {'core'}, dimensions={0}, use_global_device_ids=true | all-gather | bytes 393216 | tf_op jit(solution)/shard_map/all_gather | solution.py:145
  31.0 1.2 %shard_map.75 = bf16[256,1024]{1,0:T(8,128)(2,1)S(1)} custom-call(bf16[256,256]{1,0:T(8,128)(2,1)S(1)} %get-tuple-element.13.left_ref, bf16[512,256]{1,0:T(8,128)(2,1)S(1)} %all_gather.3.right_ref), custom_call_target="tpu_custom_call" | custom-call | tf_op jit(solution)/shard_map/pallas_call | solution.py:146
  32.2 0.1 copy.10
  32.3 34.3 %all_to_all.11 = bf16[256,8,128]{2,1,0:T(8,128)(2,1)S(1)} all-to-all(bf16[256,8,128]{2,1,0:T(8,128)(2,1)S(1)} %bitcast.20), channel_id=1, replica_groups=mesh['z_lo'=2,'y'=8,'core'=2,'x'=4,'z_hi'=4] {'x','z_hi','z_lo','y'}, dimensions={0} | all-to-all | bytes 1048576 | tf_op jit(solution)/shard_map/all_to_all | solution.py:106
  66.6 0.1 copy.14
  66.7 1.0 %shard_map.76 = bf16[512,128]{1,0:T(8,128)(2,1)} custom-call(bf16[256,1024]{1,0:T(8,128)(2,1)S(1)} %bitcast.17, bf16[512,128]{1,0:T(8,128)(2,1)S(1)} %get-tuple-element.15.pair_ref, f32[512,128]{1,0:T(8,128)S(1)} %get-tuple-element.16.gate_ref, f32[1,128]{1,0:T(1,128)S(1)} %get-tuple-element.17.gain_ref, bf16[128,128]{1,0:T(8,128)(2,1)S(1)} %get-tuple-element.18.w_out_ref), custom_call_target="tpu_custom_call" | custom-call | tf_op jit(solution)/shard_map/pallas_call | solution.py:147
  (1 shorter events, 0.0 us)

commit v3 on v2

v3 whole, which is shorter than its diff:
```python
import jax
import jax.numpy as jnp
from jax import lax
from jax.experimental import pallas as pl
from jax.experimental.pallas import tpu as pltpu
from jax.sharding import Mesh
from jax.sharding import PartitionSpec as P

AXES = ("z_lo", "y", "core", "x", "z_out", "z_in")
F32, BF16 = jnp.float32, jnp.bfloat16


def iota(shape, axis):
    return lax.broadcasted_iota(jnp.int32, shape, axis)


def project(*refs):
    sources, (send_ref, gate_ref, pair_ref, gain_mid_ref, w_out_ref) = refs[:7], refs[7:12]
    mask_ref, gain_ref, w_in_ref, w_gate_ref, arrived = refs[12:]
    targets = (pair_ref, mask_ref, gain_ref, w_in_ref, w_gate_ref, gain_mid_ref, w_out_ref)
    copies = [
        pltpu.make_async_copy(source, target, arrived.at[n]) for n, (source, target) in enumerate(zip(sources, targets))
    ]
    for copy in copies:
        copy.start()
    copies[0].wait()
    copies[2].wait()
    values = pair_ref[...].astype(F32)
    center = values - jnp.mean(values, axis=-1, keepdims=True)
    spread = jnp.mean(center * center, axis=-1, keepdims=True)
    normed = (center * lax.rsqrt(spread + 1e-05) * gain_ref[...]).astype(BF16)
    for n in (1, 3, 4, 5, 6):
        copies[n].wait()
    gate_ref[...] = jax.nn.sigmoid(jnp.dot(normed, w_gate_ref[...], preferred_element_type=F32))
    place = iota((32, 512), 1)
    spread_mask = jnp.dot(
        mask_ref[...].astype(F32), (place & 31 == iota((32, 512), 0)).astype(F32), preferred_element_type=F32
    )
    row = iota((16, 512), 1) >> 5
    keeper = jnp.sum(jnp.where(row == iota((16, 512), 0), spread_mask, 0.0), axis=0, keepdims=True)
    projected = lax.dot_general(w_in_ref[...], normed, (((0,), (1,)), ((), ())), preferred_element_type=F32)
    for side in range(2):
        start = side * 256
        both = (
            jax.nn.sigmoid(projected[start : start + 128]) * projected[start + 128 : start + 256] * keeper
        )
        send_ref[:, side * 512 : side * 512 + 512] = both.astype(BF16)


def turn(blocks):
    rows, lanes = blocks.shape
    return jnp.concatenate(
        [
            jnp.concatenate([blocks[a : a + 16, b : b + 32] for a in range(0, rows, 16)], axis=1)
            for b in range(0, lanes, 32)
        ],
        axis=0,
    )


def assemble(got_ref, left_ref, right_ref):
    left_ref[...] = turn(got_ref[:, :512])
    to, source = iota((256, 256), 0), iota((256, 256), 1)
    moved = ((to & 15) * 16 + (to >> 4) == source).astype(BF16)
    right_ref[...] = jnp.dot(moved, turn(got_ref[:, 512:]), preferred_element_type=F32).astype(BF16)


def multiply(left_ref, right_ref, send_ref):
    right = jnp.concatenate(
        [right_ref[parity * 256 + q * 16 : parity * 256 + q * 16 + 16, :] for q in range(16) for parity in range(2)],
        axis=0,
    )
    summed = lax.dot_general(left_ref[...], right, (((1,), (1,)), ((), ())), preferred_element_type=F32)
    send_ref[...] = turn(summed.astype(BF16))


def finish(got_ref, pair_ref, gate_ref, gain_ref, w_out_ref, out_ref):
    same = iota((128, 128), 0) == iota((128, 128), 1)
    gain = jnp.sum(jnp.where(same, gain_ref[...], 0.0), axis=1, keepdims=True)
    summed = jnp.concatenate(
        [got_ref[at : at + 32, :].astype(F32) + got_ref[at + 32 : at + 64, :].astype(F32) for at in range(0, 256, 64)], axis=0
    )
    center = summed - jnp.mean(summed, axis=0, keepdims=True)
    spread = jnp.mean(center * center, axis=0, keepdims=True)
    middle = (center * lax.rsqrt(spread + 1e-05) * gain).astype(BF16)
    update = lax.dot_general(middle, w_out_ref[...], (((0,), (0,)), ((), ())), preferred_element_type=F32)
    out_ref[...] = (pair_ref[...].astype(F32) + gate_ref[...] * update).astype(BF16)


def kernel(body, out_shape, **more):
    return pl.pallas_call(
        body, out_shape=out_shape, compiler_params=pltpu.CompilerParams(vmem_limit_bytes=32 * 1024 * 1024), **more
    )


def exchange(rows, axes):
    many, lanes = rows.shape
    return lax.all_to_all(rows.reshape(many, lanes // 128, 128), axes, 0, 0).reshape(many, lanes)


def shards(pair, pair_mask, gain_in, w_in, w_gate, gain_mid, w_out):
    array = jax.ShapeDtypeStruct
    sides, gate, tokens, gain_mid, w_out = kernel(
        project,
        (
            array((128, 1024), BF16),
            array((512, 128), F32),
            array((512, 128), BF16),
            array((1, 128), F32),
            array((128, 128), BF16),
        ),
        in_specs=[pl.BlockSpec(memory_space=pltpu.HBM)] * 7,
        scratch_shapes=[
            pltpu.VMEM((16, 32), jnp.int32),
            pltpu.VMEM((1, 128), F32),
            pltpu.VMEM((128, 512), BF16),
            pltpu.VMEM((128, 128), BF16),
            pltpu.SemaphoreType.DMA((7,)),
        ],
    )(
        *(
            pltpu.with_memory_space_constraint(value, pltpu.HBM)
            for value in (
                pair.reshape(512, 128),
                pair_mask,
                gain_in.reshape(1, 128),
                w_in,
                w_gate,
                gain_mid.reshape(1, 128),
                w_out,
            )
        )
    )
    left, right = kernel(assemble, (array((256, 256), BF16), array((256, 256), BF16)))(
        exchange(sides, ("x", "z_in", "z_lo", "y"))
    )
    right = lax.all_gather(right, "core", axis=0, tiled=True)
    parts = kernel(multiply, array((256, 512), BF16))(left, right)
    out = kernel(finish, array((512, 128), BF16))(exchange(parts, ("x", "z_out", "z_in", "z_lo", "y")), tokens, gate, gain_mid, w_out)
    return out.reshape(pair.shape)


def solution(mesh):
    fine = Mesh(mesh.devices.reshape(2, 8, 2, 4, 2, 2), AXES)
    pair_spec = P(AXES[:3], AXES[3:], None)
    in_specs = (pair_spec, P(AXES[:3], AXES[3:]), P(), P(), P(), P(), P())
    return jax.shard_map(shards, mesh=fine, in_specs=in_specs, out_specs=pair_spec, check_vma=False)
```

time: 68.4 us -> 65.8 us (0.962)
  blocking collectives: 63.2 us -> 61.6 us
  Pallas kernels: 4.11 us -> 3.31 us
    all_to_all x2, blocking collectives: 58.5 us -> 57.3 us  [exchange(): lax.all_to_all(rows.reshape(many, lanes // 128, 128), axes, 0, 0)]
    pallas_call x2, Pallas kernels: 2.78 us -> 2.01 us  [the longest x1 1.54 us: shards(): kernel(project, (array((128, 1024), BF16), array((512, 128), F32), array(...]
where the time goes in v3:
time: 65.8 us; the launch traced here: 65.2 us
  blocking collectives  61.6 us (94%)
  Pallas kernels  3.31 us (5%)
    all_to_all x2, blocking collectives, exchange(): lax.all_to_all(rows.reshape(many, lanes // 128, 128), axes, 0, 0)  57.3 us
    all_gather x1, blocking collectives, shards(): right = lax.all_gather(right, 'core', axis=0, tiled=True)  4.3 us
    pallas_call x1, Pallas kernels, shards(): kernel(project, (array((128, 1024), BF16), array((512, 128), F32), array(...  1.54 us

profile of v3, /device:TPU:1, one launch (start us, length us, event | category | flops | bytes accessed | tf_op | source)
XLA Modules:
  0.0 65.2 jit_solution(9098316306749740833)
XLA Ops:
  0.0 1.5 %shard_map.73 = (bf16[128,1024]{1,0:T(8,128)(2,1)S(1)}, f32[512,128]{1,0:T(8,128)S(1)}, bf16[512,128]{1,0:T(8,128)(2,1)S(1)}, f32[1,128]{1,0:T(1,128)S(1)}, bf16[128,128]{1,0:T(8,128)(2,1)S(1)}) custom-call(bf16[512,128]{1,0:T(8,128)(2,1)} %bitcast.20, s32[16,32]{1,0:T(8,128)} %refs_1_.1, f32[1,128]{1,0:T(1,128)} %bitcast.21, bf16[128,512]{1,0:T(8,128)(2,1)} %refs_3_.1, ...), custom_call_target="tpu_custom_call" | custom-call | tf_op jit(solution)/shard_map/pallas_call | solution.py:103
  1.6 31.5 %all_to_all.10 = bf16[128,8,128]{2,1,0:T(8,128)(2,1)S(1)} all-to-all(bf16[128,8,128]{2,1,0:T(8,128)(2,1)S(1)} %bitcast.17), channel_id=1, replica_groups=mesh['z_lo'=2,'y'=8,'core'=2,'x'=4,'z_out'=2,'z_in'=2] {'x','z_in','z_lo..., dimensions={0} | all-to-all | bytes 524288 | tf_op jit(solution)/shard_map/all_to_all | solution.py:98
  33.2 0.3 shard_map.74
  33.5 4.3 %all_gather.3.right_ref = bf16[512,256]{1,0:T(8,128)(2,1)S(1)} all-gather(bf16[256,256]{1,0:T(8,128)(2,1)S(1)} %get-tuple-element.14), channel_id=1, replica_groups=mesh['z_lo'=2,'y'=8,'core'=2,'x'=4,'z_out'=2,'z_in'=2] {'core'}, dimensions={0}, use_global_device_ids=true | all-gather | bytes 393216 | tf_op jit(solution)/shard_map/all_gather | solution.py:137
  37.8 0.5 shard_map.75
  38.3 0.1 reshape.29
  38.3 25.8 %all_to_all.11 = bf16[256,4,128]{2,1,0:T(4,128)(2,1)S(1)} all-to-all(bf16[256,4,128]{2,1,0:T(4,128)(2,1)S(1)} %reshape.29), channel_id=1, replica_groups=mesh['z_lo'=2,'y'=8,'core'=2,'x'=4,'z_out'=2,'z_in'=2] {'x','z_out','z_i..., dimensions={0} | all-to-all | bytes 524288 | tf_op jit(solution)/shard_map/all_to_all | solution.py:98
  64.2 1.0 %shard_map.76 = bf16[512,128]{1,0:T(8,128)(2,1)} custom-call(bf16[256,512]{1,0:T(8,128)(2,1)S(1)} %bitcast.15, bf16[512,128]{1,0:T(8,128)(2,1)S(1)} %get-tuple-element.15.pair_ref, f32[512,128]{1,0:T(8,128)S(1)} %get-tuple-element.16.gate_ref, f32[1,128]{1,0:T(1,128)S(1)} %get-tuple-element.17.gain_ref, bf16[128,128]{1,0:T(8,128)(2,1)S(1)} %get-tuple-element.18.w_out_ref), custom_call_target="tpu_custom_call" | custom-call | tf_op jit(solution)/shard_map/pallas_call | solution.py:139
  (3 shorter events, 0.1 us)

commit v4 on v3

--- a/solution.py
+++ b/solution.py
@@ -6,7 +6,7 @@
 from jax.sharding import Mesh
 from jax.sharding import PartitionSpec as P
 
-AXES = ("z_lo", "y", "core", "x", "z_out", "z_in")
+AXES = ("z_lo", "y", "core", "x1", "x0", "z_out", "z_in")
 F32, BF16 = jnp.float32, jnp.bfloat16
 
 
@@ -67,7 +67,11 @@
 
 def multiply(left_ref, right_ref, send_ref):
     right = jnp.concatenate(
-        [right_ref[parity * 256 + q * 16 : parity * 256 + q * 16 + 16, :] for q in range(16) for parity in range(2)],
+        [
+            right_ref[parity * 256 + q * 16 : parity * 256 + q * 16 + 16, :]
+            for q in (x1 * 8 + x0 * 4 + z for x0 in range(2) for out in range(2) for x1 in range(2) for z in (out * 2, out * 2 + 1))
+            for parity in range(2)
+        ],
         axis=0,
     )
     summed = lax.dot_general(left_ref[...], right, (((1,), (1,)), ((), ())), preferred_element_type=F32)
@@ -78,7 +82,11 @@
     same = iota((128, 128), 0) == iota((128, 128), 1)
     gain = jnp.sum(jnp.where(same, gain_ref[...], 0.0), axis=1, keepdims=True)
     summed = jnp.concatenate(
-        [got_ref[at : at + 32, :].astype(F32) + got_ref[at + 32 : at + 64, :].astype(F32) for at in range(0, 256, 64)], axis=0
+        [
+            got_ref[at : at + 32, :].astype(F32) + got_ref[at + 64 : at + 96, :].astype(F32)
+            for at in (x0 * 128 + x1 * 32 for x1 in range(2) for x0 in range(2))
+        ],
+        axis=0,
     )
     center = summed - jnp.mean(summed, axis=0, keepdims=True)
     spread = jnp.mean(center * center, axis=0, keepdims=True)
@@ -132,16 +140,16 @@
         )
     )
     left, right = kernel(assemble, (array((256, 256), BF16), array((256, 256), BF16)))(
-        exchange(sides, ("x", "z_in", "z_lo", "y"))
+        exchange(sides, ("x1", "x0", "z_in", "z_lo", "y"))
     )
     right = lax.all_gather(right, "core", axis=0, tiled=True)
     parts = kernel(multiply, array((256, 512), BF16))(left, right)
-    out = kernel(finish, array((512, 128), BF16))(exchange(parts, ("x", "z_out", "z_in", "z_lo", "y")), tokens, gate, gain_mid, w_out)
+    out = kernel(finish, array((512, 128), BF16))(exchange(parts, ("x0", "z_out", "x1", "z_in", "z_lo", "y")), tokens, gate, gain_mid, w_out)
     return out.reshape(pair.shape)
 
 
 def solution(mesh):
-    fine = Mesh(mesh.devices.reshape(2, 8, 2, 4, 2, 2), AXES)
+    fine = Mesh(mesh.devices.reshape(2, 8, 2, 2, 2, 2, 2), AXES)
     pair_spec = P(AXES[:3], AXES[3:], None)
     in_specs = (pair_spec, P(AXES[:3], AXES[3:]), P(), P(), P(), P(), P())
     return jax.shard_map(shards, mesh=fine, in_specs=in_specs, out_specs=pair_spec, check_vma=False)

time: 65.8 us -> 65.8 us (level)
  no operation moved by 1% of the time
where the time goes in v4:
time: 65.8 us; the launch traced here: 64.9 us
  blocking collectives  61.4 us (93%)
  Pallas kernels  3.31 us (5%)
    all_to_all x2, blocking collectives, exchange(): lax.all_to_all(rows.reshape(many, lanes // 128, 128), axes, 0, 0)  57.1 us
    all_gather x1, blocking collectives, shards(): right = lax.all_gather(right, 'core', axis=0, tiled=True)  4.3 us
    pallas_call x1, Pallas kernels, shards(): kernel(project, (array((128, 1024), BF16), array((512, 128), F32), array(...  1.54 us

profile of v4, /device:TPU:1, one launch (start us, length us, event | category | flops | bytes accessed | tf_op | source)
XLA Modules:
  0.0 64.9 jit_solution(2615596181027032493)
XLA Ops:
  0.0 1.5 %shard_map.73 = (bf16[128,1024]{1,0:T(8,128)(2,1)S(1)}, f32[512,128]{1,0:T(8,128)S(1)}, bf16[512,128]{1,0:T(8,128)(2,1)S(1)}, f32[1,128]{1,0:T(1,128)S(1)}, bf16[128,128]{1,0:T(8,128)(2,1)S(1)}) custom-call(bf16[512,128]{1,0:T(8,128)(2,1)} %bitcast.20, s32[16,32]{1,0:T(8,128)} %refs_1_.1, f32[1,128]{1,0:T(1,128)} %bitcast.21, bf16[128,512]{1,0:T(8,128)(2,1)} %refs_3_.1, ...), custom_call_target="tpu_custom_call" | custom-call | tf_op jit(solution)/shard_map/pallas_call | solution.py:111
  1.6 31.5 %all_to_all.10 = bf16[128,8,128]{2,1,0:T(8,128)(2,1)S(1)} all-to-all(bf16[128,8,128]{2,1,0:T(8,128)(2,1)S(1)} %bitcast.17), channel_id=1, replica_groups=mesh['z_lo'=2,'y'=8,'core'=2,'x1'=2,'x0'=2,'z_out'=2,'z_in'=2] {'x1','x0..., dimensions={0} | all-to-all | bytes 524288 | tf_op jit(solution)/shard_map/all_to_all | solution.py:106
  33.2 0.3 shard_map.74
  33.5 4.3 %all_gather.3.right_ref = bf16[512,256]{1,0:T(8,128)(2,1)S(1)} all-gather(bf16[256,256]{1,0:T(8,128)(2,1)S(1)} %get-tuple-element.14), channel_id=1, replica_groups=mesh['z_lo'=2,'y'=8,'core'=2,'x1'=2,'x0'=2,'z_out'=2,'z_in'=2] {'core'}, dimensions={0}, use_global_device_ids=true | all-gather | bytes 393216 | tf_op jit(solution)/shard_map/all_gather | solution.py:145
  37.8 0.5 shard_map.75
  38.3 0.1 reshape.29
  38.3 25.5 %all_to_all.11 = bf16[256,4,128]{2,1,0:T(4,128)(2,1)S(1)} all-to-all(bf16[256,4,128]{2,1,0:T(4,128)(2,1)S(1)} %reshape.29), channel_id=1, replica_groups=mesh['z_lo'=2,'y'=8,'core'=2,'x1'=2,'x0'=2,'z_out'=2,'z_in'=2] {'x0','z_..., dimensions={0} | all-to-all | bytes 524288 | tf_op jit(solution)/shard_map/all_to_all | solution.py:106
  63.9 1.0 %shard_map.76 = bf16[512,128]{1,0:T(8,128)(2,1)} custom-call(bf16[256,512]{1,0:T(8,128)(2,1)S(1)} %bitcast.15, bf16[512,128]{1,0:T(8,128)(2,1)S(1)} %get-tuple-element.15.pair_ref, f32[512,128]{1,0:T(8,128)S(1)} %get-tuple-element.16.gate_ref, f32[1,128]{1,0:T(1,128)S(1)} %get-tuple-element.17.gain_ref, bf16[128,128]{1,0:T(8,128)(2,1)S(1)} %get-tuple-element.18.w_out_ref), custom_call_target="tpu_custom_call" | custom-call | tf_op jit(solution)/shard_map/pallas_call | solution.py:147
  (3 shorter events, 0.1 us)

commit v5 on v4

--- a/solution.py
+++ b/solution.py
@@ -8,6 +8,10 @@
 
 AXES = ("z_lo", "y", "core", "x1", "x0", "z_out", "z_in")
 F32, BF16 = jnp.float32, jnp.bfloat16
+
+
+def sigmoid(values):
+    return 0.5 * jnp.tanh(0.5 * values) + 0.5
 
 
 def iota(shape, axis):
@@ -31,7 +35,7 @@
     normed = (center * lax.rsqrt(spread + 1e-05) * gain_ref[...]).astype(BF16)
     for n in (1, 3, 4, 5, 6):
         copies[n].wait()
-    gate_ref[...] = jax.nn.sigmoid(jnp.dot(normed, w_gate_ref[...], preferred_element_type=F32))
+    gate_ref[...] = sigmoid(jnp.dot(normed, w_gate_ref[...], preferred_element_type=F32))
     place = iota((32, 512), 1)
     spread_mask = jnp.dot(
         mask_ref[...].astype(F32), (place & 31 == iota((32, 512), 0)).astype(F32), preferred_element_type=F32
@@ -42,7 +46,7 @@
     for side in range(2):
         start = side * 256
         both = (
-            jax.nn.sigmoid(projected[start : start + 128]) * projected[start + 128 : start + 256] * keeper
+            sigmoid(projected[start : start + 128]) * projected[start + 128 : start + 256] * keeper
         )
         send_ref[:, side * 512 : side * 512 + 512] = both.astype(BF16)
 

time: 65.8 us -> 65.8 us (level)
  no operation moved by 1% of the time
where the time goes in v5:
time: 65.8 us; the launch traced here: 64.9 us
  blocking collectives  61.4 us (93%)
  Pallas kernels  3.31 us (5%)
    all_to_all x2, blocking collectives, exchange(): lax.all_to_all(rows.reshape(many, lanes // 128, 128), axes, 0, 0)  57.1 us
    all_gather x1, blocking collectives, shards(): right = lax.all_gather(right, 'core', axis=0, tiled=True)  4.3 us
    pallas_call x1, Pallas kernels, shards(): kernel(project, (array((128, 1024), BF16), array((512, 128), F32), array(...  1.54 us

profile of v5, /device:TPU:1, one launch (start us, length us, event | category | flops | bytes accessed | tf_op | source)
XLA Modules:
  0.0 64.9 jit_solution(1250468110565145514)
XLA Ops:
  0.0 1.5 %shard_map.73 = (bf16[128,1024]{1,0:T(8,128)(2,1)S(1)}, f32[512,128]{1,0:T(8,128)S(1)}, bf16[512,128]{1,0:T(8,128)(2,1)S(1)}, f32[1,128]{1,0:T(1,128)S(1)}, bf16[128,128]{1,0:T(8,128)(2,1)S(1)}) custom-call(bf16[512,128]{1,0:T(8,128)(2,1)} %bitcast.20, s32[16,32]{1,0:T(8,128)} %refs_1_.1, f32[1,128]{1,0:T(1,128)} %bitcast.21, bf16[128,512]{1,0:T(8,128)(2,1)} %refs_3_.1, ...), custom_call_target="tpu_custom_call" | custom-call | tf_op jit(solution)/shard_map/pallas_call | solution.py:115
  1.6 31.5 %all_to_all.10 = bf16[128,8,128]{2,1,0:T(8,128)(2,1)S(1)} all-to-all(bf16[128,8,128]{2,1,0:T(8,128)(2,1)S(1)} %bitcast.17), channel_id=1, replica_groups=mesh['z_lo'=2,'y'=8,'core'=2,'x1'=2,'x0'=2,'z_out'=2,'z_in'=2] {'x1','x0..., dimensions={0} | all-to-all | bytes 524288 | tf_op jit(solution)/shard_map/all_to_all | solution.py:110
  33.2 0.3 shard_map.74
  33.5 4.3 %all_gather.3.right_ref = bf16[512,256]{1,0:T(8,128)(2,1)S(1)} all-gather(bf16[256,256]{1,0:T(8,128)(2,1)S(1)} %get-tuple-element.14), channel_id=1, replica_groups=mesh['z_lo'=2,'y'=8,'core'=2,'x1'=2,'x0'=2,'z_out'=2,'z_in'=2] {'core'}, dimensions={0}, use_global_device_ids=true | all-gather | bytes 393216 | tf_op jit(solution)/shard_map/all_gather | solution.py:149
  37.8 0.5 shard_map.75
  38.3 0.1 reshape.29
  38.3 25.5 %all_to_all.11 = bf16[256,4,128]{2,1,0:T(4,128)(2,1)S(1)} all-to-all(bf16[256,4,128]{2,1,0:T(4,128)(2,1)S(1)} %reshape.29), channel_id=1, replica_groups=mesh['z_lo'=2,'y'=8,'core'=2,'x1'=2,'x0'=2,'z_out'=2,'z_in'=2] {'x0','z_..., dimensions={0} | all-to-all | bytes 524288 | tf_op jit(solution)/shard_map/all_to_all | solution.py:110
  63.9 1.0 %shard_map.76 = bf16[512,128]{1,0:T(8,128)(2,1)} custom-call(bf16[256,512]{1,0:T(8,128)(2,1)S(1)} %bitcast.15, bf16[512,128]{1,0:T(8,128)(2,1)S(1)} %get-tuple-element.15.pair_ref, f32[512,128]{1,0:T(8,128)S(1)} %get-tuple-element.16.gate_ref, f32[1,128]{1,0:T(1,128)S(1)} %get-tuple-element.17.gain_ref, bf16[128,128]{1,0:T(8,128)(2,1)S(1)} %get-tuple-element.18.w_out_ref), custom_call_target="tpu_custom_call" | custom-call | tf_op jit(solution)/shard_map/pallas_call | solution.py:151
  (3 shorter events, 0.1 us)

commit v6 on v5

--- a/solution.py
+++ b/solution.py
@@ -87,8 +87,8 @@
     gain = jnp.sum(jnp.where(same, gain_ref[...], 0.0), axis=1, keepdims=True)
     summed = jnp.concatenate(
         [
-            got_ref[at : at + 32, :].astype(F32) + got_ref[at + 64 : at + 96, :].astype(F32)
-            for at in (x0 * 128 + x1 * 32 for x1 in range(2) for x0 in range(2))
+            got_ref[at : at + 16, :].astype(F32) + got_ref[at + 64 : at + 80, :].astype(F32)
+            for at in (x0 * 128 + x1 * 32 + z_in * 16 for z_in in range(2) for x1 in range(2) for x0 in range(2))
         ],
         axis=0,
     )
@@ -144,7 +144,7 @@
         )
     )
     left, right = kernel(assemble, (array((256, 256), BF16), array((256, 256), BF16)))(
-        exchange(sides, ("x1", "x0", "z_in", "z_lo", "y"))
+        exchange(sides, ("z_in", "x1", "x0", "z_lo", "y"))
     )
     right = lax.all_gather(right, "core", axis=0, tiled=True)
     parts = kernel(multiply, array((256, 512), BF16))(left, right)

time: 65.8 us -> 66.3 us (level)
  no operation moved by 1% of the time
where the time goes in v6:
time: 66.3 us; the launch traced here: 65.3 us
  blocking collectives  61.8 us (93%)
  Pallas kernels  3.31 us (5%)
    all_to_all x2, blocking collectives, exchange(): lax.all_to_all(rows.reshape(many, lanes // 128, 128), axes, 0, 0)  57.5 us
    all_gather x1, blocking collectives, shards(): right = lax.all_gather(right, 'core', axis=0, tiled=True)  4.3 us
    pallas_call x1, Pallas kernels, shards(): kernel(project, (array((128, 1024), BF16), array((512, 128), F32), array(...  1.54 us

profile of v6, /device:TPU:1, one launch (start us, length us, event | category | flops | bytes accessed | tf_op | source)
XLA Modules:
  0.0 65.3 jit_solution(18399528921684206584)
XLA Ops:
  0.0 1.5 %shard_map.73 = (bf16[128,1024]{1,0:T(8,128)(2,1)S(1)}, f32[512,128]{1,0:T(8,128)S(1)}, bf16[512,128]{1,0:T(8,128)(2,1)S(1)}, f32[1,128]{1,0:T(1,128)S(1)}, bf16[128,128]{1,0:T(8,128)(2,1)S(1)}) custom-call(bf16[512,128]{1,0:T(8,128)(2,1)} %bitcast.20, s32[16,32]{1,0:T(8,128)} %refs_1_.1, f32[1,128]{1,0:T(1,128)} %bitcast.21, bf16[128,512]{1,0:T(8,128)(2,1)} %refs_3_.1, ...), custom_call_target="tpu_custom_call" | custom-call | tf_op jit(solution)/shard_map/pallas_call | solution.py:115
  1.6 31.5 %all_to_all.10 = bf16[128,8,128]{2,1,0:T(8,128)(2,1)S(1)} all-to-all(bf16[128,8,128]{2,1,0:T(8,128)(2,1)S(1)} %bitcast.17), channel_id=1, replica_groups=mesh['z_lo'=2,'y'=8,'core'=2,'x1'=2,'x0'=2,'z_out'=2,'z_in'=2] {'z_in','..., dimensions={0} | all-to-all | bytes 524288 | tf_op jit(solution)/shard_map/all_to_all | solution.py:110
  33.2 0.3 shard_map.74
  33.5 4.3 %all_gather.3.right_ref = bf16[512,256]{1,0:T(8,128)(2,1)S(1)} all-gather(bf16[256,256]{1,0:T(8,128)(2,1)S(1)} %get-tuple-element.14), channel_id=1, replica_groups=mesh['z_lo'=2,'y'=8,'core'=2,'x1'=2,'x0'=2,'z_out'=2,'z_in'=2] {'core'}, dimensions={0}, use_global_device_ids=true | all-gather | bytes 393216 | tf_op jit(solution)/shard_map/all_gather | solution.py:149
  37.8 0.5 shard_map.75
  38.3 0.1 reshape.29
  38.3 26.0 %all_to_all.11 = bf16[256,4,128]{2,1,0:T(4,128)(2,1)S(1)} all-to-all(bf16[256,4,128]{2,1,0:T(4,128)(2,1)S(1)} %reshape.29), channel_id=1, replica_groups=mesh['z_lo'=2,'y'=8,'core'=2,'x1'=2,'x0'=2,'z_out'=2,'z_in'=2] {'x0','z_..., dimensions={0} | all-to-all | bytes 524288 | tf_op jit(solution)/shard_map/all_to_all | solution.py:110
  64.4 1.0 %shard_map.76 = bf16[512,128]{1,0:T(8,128)(2,1)} custom-call(bf16[256,512]{1,0:T(8,128)(2,1)S(1)} %bitcast.15, bf16[512,128]{1,0:T(8,128)(2,1)S(1)} %get-tuple-element.15.pair_ref, f32[512,128]{1,0:T(8,128)S(1)} %get-tuple-element.16.gate_ref, f32[1,128]{1,0:T(1,128)S(1)} %get-tuple-element.17.gain_ref, bf16[128,128]{1,0:T(8,128)(2,1)S(1)} %get-tuple-element.18.w_out_ref), custom_call_target="tpu_custom_call" | custom-call | tf_op jit(solution)/shard_map/pallas_call | solution.py:151
  (3 shorter events, 0.1 us)
